TPU v7x, 128 devices: a whole 4x4x4 slice. The times are simulated.
128 devices in a mesh: tm: 32 (over z, x, y_hi), rows: 4 (over y_lo, core).
Axes of the slice: x: 4, y: 4 (y_hi: 2, y_lo: 2; y = y_hi * 2 + y_lo), z: 4, core: 2. Of those that a mesh axis runs over, the one named last changes fastest.
Arguments:
- video: bfloat16 [256, 32, 128, 128], P('tm', 'rows'), may hold values from -36 to 50
- conv_weight: bfloat16 [3, 3, 3, 128, 256], replicated, may hold values from -0.109375 to 0.109375
- norm_gain: float32 [256], replicated, may hold values from 0.5 to 1.5
- norm_bias: float32 [256], replicated, may hold values from -3 to 3
Outputs:
- patch_tokens: bfloat16 [16, 64, 256, 1024], P('rows', 'tm')
All inputs are finite; a program needn't handle non-finite values.
Results may differ from a plain program's by a relative error of at most 0.0049.
Values may be sent and summed in bfloat16 or wider, within the bound.
A program may use at most 128 MiB of HBM per device.

v0:
```python
import jax
import jax.numpy as jnp
from jax import lax
from jax.sharding import PartitionSpec as P

GROUPS = 32
inv_root = 0.7071067811865476


def from_partner(block, axis, distance):
    count = lax.axis_size(axis)
    route = []
    for low in range(count):
        high = low | 1 << distance
        if high != low and high < count:
            route += [(low, high), (high, low)]
    return lax.ppermute(block, axis, route)


def shifted(block, axis, distance):
    devices = range(lax.axis_size(axis))
    route = [(i - distance, i) for i in devices if i - distance in devices]
    return lax.ppermute(block, axis, route)


def padded_2(cells, sides, width):
    for axis, dim in sides:
        count = lax.axis_size(axis)
        ends = count - 1
        head = lax.slice_in_dim(cells, 0, width, axis=dim)
        tail = lax.slice_in_dim(cells, cells.shape[dim] - width, cells.shape[dim], axis=dim)
        cells = jnp.concatenate(
            [
                lax.ppermute(tail, axis, [(i, (i + 1) % count) for i in range(ends)]),
                cells,
                lax.ppermute(head, axis, [((i + 1) % count, i) for i in range(ends)]),
            ],
            axis=dim,
        )
    return cells


def per_device(video, conv_weight, norm_gain, norm_bias):
    frames, height, width, channels = video.shape
    tm_count = lax.axis_size("tm")
    current = video.astype(jnp.float32)
    position = lax.axis_index("tm")
    for bit_number in range(3):
        partner = from_partner(current, "tm", bit_number)
        is_upper = position >> bit_number & 1 == 1
        current = jnp.where(
            is_upper, (partner - current) * inv_root, (current + partner) * inv_root
        )
    wavelet = current.astype(jnp.bfloat16)
    last_frames = wavelet[frames - 2 :]
    earlier = shifted(last_frames, "tm", 1)
    extended = jnp.concatenate([earlier, wavelet], axis=0)
    with_rows = padded_2(extended, (("rows", 1),), 1)
    padded = jnp.pad(with_rows, ((0, 0), (0, 0), (1, 1), (0, 0)))
    convolved = lax.conv_general_dilated(
        padded[None],
        conv_weight,
        (1, 1, 1),
        "VALID",
        dimension_numbers=("NDHWC", "DHWIO", "NDHWC"),
        preferred_element_type=jnp.float32,
    )[0]
    out_frames, out_height, out_width, out_channels = convolved.shape
    group_count = GROUPS
    groups = convolved.reshape(
        out_frames, out_height, out_width, group_count, out_channels // group_count
    )
    entries = float(
        out_frames
        * out_height
        * out_width
        * (out_channels // group_count)
        * tm_count
        * lax.axis_size("rows")
    )
    local_sums = jnp.sum(groups, axis=(0, 1, 2, 4))
    group_total = lax.psum(local_sums, ("tm", "rows"))
    group_mean = group_total / entries
    centered = groups - group_mean[:, None]
    squares = lax.psum(jnp.sum(centered * centered, axis=(0, 1, 2, 4)), ("tm", "rows"))
    variance = squares / entries
    normed = (centered / jnp.sqrt(variance + 1e-05)[:, None]).reshape(
        out_frames, out_height, out_width, out_channels
    )
    activated = jax.nn.silu(normed * norm_gain + norm_bias).astype(jnp.bfloat16)
    arranged = activated.reshape(
        out_frames, out_height // 2, 2, out_width // 2, 2, out_channels
    ).transpose(1, 3, 0, 2, 4, 5)
    arranged = arranged.reshape(out_height // 2, out_width // 2, out_frames, 4 * out_channels)
    return lax.all_to_all(arranged, "tm", split_axis=1, concat_axis=2, tiled=True)


def solution(mesh):
    placed = (P("tm", "rows", None, None), P(), P(), P())
    return jax.shard_map(
        per_device,
        mesh=mesh,
        in_specs=placed,
        out_specs=P("rows", "tm", None, None),
        check_vma=False,
    )
```

profile of v0, /device:TPU:0, one launch (start us, length us, event | category | flops | bytes accessed | tf_op | source)
XLA Modules:
  0.0 597.1 jit_solution(17662172223809165032)
XLA Ops:
  0.0 0.0 copy-start
  0.0 4.3 convert_element_type.12
  4.3 3.3 collective-permute-start
  7.5 90.9 %collective-permute-done = f32[8,8,128,128]{3,2,1,0:T(8,128)} collective-permute-done((f32[8,8,128,128]{3,2,1,0:T(8,128)}, f32[8,8,128,128]{3,2,1,0:T(8,128)}, u32[]{:S(2)}, u32[]{:S(2)}) %collective-permute-start) | collective-permute-done | bytes 4194336 | tf_op jit(solution)/shard_map/ppermute | solution.py:17
  98.4 5.9 multiply_select_fusion.1
  104.3 1.5 collective-permute-start.1
  105.9 90.2 %collective-permute-done.1 = f32[8,8,128,128]{3,2,1,0:T(8,128)} collective-permute-done((f32[8,8,128,128]{3,2,1,0:T(8,128)}, f32[8,8,128,128]{3,2,1,0:T(8,128)}, u32[]{:S(2)}, u32[]{:S(2)}) %collective-permute-start.1) | collective-permute-done | bytes 4194336 | tf_op jit(solution)/shard_map/ppermute | solution.py:17
  196.1 6.9 %multiply_select_fusion = f32[8,8,128,128]{3,2,1,0:T(8,128)} fusion(f32[8,8,128,128]{3,2,1,0:T(8,128)} %multiply_select_fusion.1, f32[8,8,128,128]{3,2,1,0:T(8,128)} %collective-permute-done.1, pred[]{:T(512)S(6)} %eq.10), kind=kLoop, calls=%fused_computation.15 | loop fusion | flops 5242880 | bytes 12582913 | tf_op jit(solution)/shard_map/jit(_where)/select_n | solution.py:51
  203.0 3.0 collective-permute-start.2
  206.1 89.3 %collective-permute-done.2 = f32[8,8,128,128]{3,2,1,0:T(8,128)} collective-permute-done((f32[8,8,128,128]{3,2,1,0:T(8,128)}, f32[8,8,128,128]{3,2,1,0:T(8,128)}, u32[]{:S(2)}, u32[]{:S(2)}) %collective-permute-start.2) | collective-permute-done | bytes 4194336 | tf_op jit(solution)/shard_map/ppermute | solution.py:17
  295.4 4.5 select_convert_fusion
  299.9 5.1 collective-permute-start.3
  305.1 8.4 %collective-permute-done.3 = bf16[2,8,128,128]{3,2,1,0:T(8,128)(2,1)S(1)} collective-permute-done((bf16[2,8,128,128]{3,2,1,0:T(8,128)(2,1)S(1)}, bf16[2,8,128,128]{3,2,1,0:T(8,128)(2,1)S(1)}, u32[]{:S(2)}, u32[]{:S(2)}) %collective-permute-start.3) | collective-permute-done | bytes 524320 | tf_op jit(solution)/shard_map/ppermute | solution.py:23
  313.5 0.1 pad_maximum_fusion.1
  313.5 1.3 collective-permute-start.4
  314.9 1.3 collective-permute-start.5
  316.2 0.0 collective-permute-done.4
  316.2 3.1 collective-permute-done.5
  319.3 2.1 fusion.13
  321.4 2.0 pad.5
  323.4 6.9 %reshape.19 = bf16[10,10,1,8,17,128]{5,4,3,1,0,2:T(8,128)(2,1)} reshape(bf16[10,10,1,136,128]{4,3,1,0,2:T(8,128)(2,1)} %pad.5) | data formatting | bytes 6963200 | tf_op jit(solution)/shard_map/conv_general_dilated | solution.py:60
  330.4 3.0 copy.29
  333.4 0.1 slice.15
  333.5 0.0 copy-done
  333.5 0.0 copy-done.3
  333.5 19.0 %select_reduce_fusion.1 = (f32[256]{0:T(256)S(1)}, f32[8,8,8,17,256]{4,2,3,1,0:T(8,128)}) fusion(pred[8,17]{0,1:T(8,128)(4,1)S(1)} %copy-done.3, bf16[3,3,3,128,256]{4,3,2,1,0:T(8,128)(2,1)S(1)} %copy-done, bf16[10,10,1,7,2,128]{5,3,4,1,0,2:T(8,128)(2,1)S(1)} %slice.15, bf16[10,10,1,8,17,128]{5,3,4,1,0,2:T(8,128)(2,1)S(1)} %copy.29), kind=kOutput, calls=%fused_computation.3 | convolution fusion | flops 15419842560 | bytes 14523528 | tf_op jit(solution)/shard_map/conv_general_dilated | solution.py:60
  352.6 0.1 reduce_sum.24
  352.7 0.1 reduce_sum.25
  352.8 75.9 %psum.14 = f32[32]{0:T(128)S(1)} all-reduce(f32[32]{0:T(128)S(1)} %reduce_sum.25), channel_id=1, replica_groups=mesh['tm'=32,'rows'=4] {'tm','rows'}, use_global_device_ids=true, to_apply=%region_2.3 | all-reduce | flops 32 | bytes 256 | tf_op jit(solution)/shard_map/psum | solution.py:82
  428.7 0.1 sub.31
  428.8 0.1 sub.32
  428.8 0.0 copy-start.2
  428.9 6.3 %copy.30 = f32[8,8,8,17,256]{4,1,3,2,0:T(8,128)S(1)} copy(f32[8,8,8,17,256]{4,2,3,1,0:T(8,128)} %get-tuple-element.8) | data formatting | bytes 17825792 | tf_op jit(solution)/shard_map/conv_general_dilated | solution.py:60
  435.2 1.5 select_reduce_fusion
  436.8 4.1 slice.16
  440.8 0.1 reduce_sum.36
  440.9 0.1 reduce_sum.37
  441.0 0.0 copy-start.4
  441.0 0.0 copy-start.5
  441.0 11.5 %copy.31 = f32[8,8,1,128,256]{4,0,3,1,2:T(8,128)} copy(f32[8,8,1,128,256]{4,1,3,0,2:T(8,128)} %slice.16) | data formatting | bytes 16777216 | tf_op jit(solution)/shard_map/conv_general_dilated | solution.py:60
  452.5 62.4 %psum.15 = f32[32]{0:T(128)S(1)} all-reduce(f32[32]{0:T(128)S(1)} %reduce_sum.37), channel_id=1, replica_groups=mesh['tm'=32,'rows'=4] {'tm','rows'}, use_global_device_ids=true, to_apply=%region_5.6 | all-reduce | flops 32 | bytes 256 | tf_op jit(solution)/shard_map/psum | solution.py:85
  515.0 0.1 div.27
  515.0 0.1 div.28
  515.2 6.9 %fusion.5 = bf16[4,64,8,2,2,256]{5,1,4,3,0,2:T(8,128)(2,1)S(1)} fusion(f32[256]{0:T(256)S(1)} %copy-done.4, f32[256]{0:T(256)S(1)} %copy-done.5, f32[256]{0:T(256)S(1)} %div.28, f32[256]{0:T(256)S(1)} %sub.32, f32[8,4,2,64,2,256]{5,0,4,3,2,1:T(8,128)} %bitcast.27), kind=kLoop, calls=%fused_computation.17 | loop fusion | flops 18874368 | bytes 12587008 | tf_op jit(solution)/shard_map/transpose | solution.py:93
  522.0 6.4 %copy.37 = bf16[4,64,8,2,2,256]{5,4,3,2,0,1:T(2,128)(2,1)} copy(bf16[4,64,8,2,2,256]{5,1,4,3,0,2:T(8,128)(2,1)S(1)} %fusion.5) | data formatting | bytes 8388608 | tf_op jit(solution)/shard_map/reshape | solution.py:94
  528.4 7.7 %reshape.33 = bf16[4,64,8,1024]{3,2,0,1:T(8,128)(2,1)} reshape(bf16[4,64,8,2,2,256]{5,4,3,2,0,1:T(2,128)(2,1)} %copy.37) | data formatting | bytes 8388608 | tf_op jit(solution)/shard_map/reshape | solution.py:94
  536.1 58.5 %all_to_all.18 = bf16[4,64,8,1024]{3,2,0,1:T(8,128)(2,1)S(1)} all-to-all(bf16[4,64,8,1024]{3,2,0,1:T(8,128)(2,1)} %reshape.33), channel_id=1, replica_groups=mesh['tm'=32,'rows'=4] {'tm'}, dimensions={1} | all-to-all | bytes 8388608 | tf_op jit(solution)/shard_map/all_to_all | solution.py:95
  594.6 2.5 copy.52
  (9 shorter events, 0.1 us)
Async XLA Ops:
  0.0 333.5 %copy-start = (bf16[3,3,3,128,256]{4,3,2,1,0:T(8,128)(2,1)S(1)}, bf16[3,3,3,128,256]{4,3,2,1,0:T(8,128)(2,1)}, u32[]{:S(2)}) copy-start(bf16[3,3,3,128,256]{4,3,2,1,0:T(8,128)(2,1)} %param.5) | copy-start | bytes 5308420
  4.3 94.2 %collective-permute-start = (f32[8,8,128,128]{3,2,1,0:T(8,128)}, f32[8,8,128,128]{3,2,1,0:T(8,128)}, u32[]{:S(2)}, u32[]{:S(2)}) collective-permute-start(f32[8,8,128,128]{3,2,1,0:T(8,128)} %convert_element_type.12), channel_id=1, source_target_pairs={{0,4},{4,0},{8,12},{12,8},{16,20},{20,16},{24,28},{28,24},{32,36},... | collective-permute-start | bytes 12582920 | tf_op jit(solution)/shard_map/ppermute | solution.py:17
  104.3 91.8 %collective-permute-start.1 = (f32[8,8,128,128]{3,2,1,0:T(8,128)}, f32[8,8,128,128]{3,2,1,0:T(8,128)}, u32[]{:S(2)}, u32[]{:S(2)}) collective-permute-start(f32[8,8,128,128]{3,2,1,0:T(8,128)} %multiply_select_fusion.1), channel_id=1, source_target_pairs={{0,8},{8,0},{4,12},{12,4},{16,24},{24,16},{20,28},{28,20},{32,40},... | collective-permute-start | bytes 12582920 | tf_op jit(solution)/shard_map/ppermute | solution.py:17
  203.0 92.4 %collective-permute-start.2 = (f32[8,8,128,128]{3,2,1,0:T(8,128)}, f32[8,8,128,128]{3,2,1,0:T(8,128)}, u32[]{:S(2)}, u32[]{:S(2)}) collective-permute-start(f32[8,8,128,128]{3,2,1,0:T(8,128)} %multiply_select_fusion), channel_id=1, source_target_pairs={{0,16},{16,0},{4,20},{20,4},{8,24},{24,8},{12,28},{28,12},{32,48},... | collective-permute-start | bytes 12582920 | tf_op jit(solution)/shard_map/ppermute | solution.py:17
  299.9 13.5 %collective-permute-start.3 = (bf16[2,8,128,128]{3,2,1,0:T(8,128)(2,1)S(1)}, bf16[2,8,128,128]{3,2,1,0:T(8,128)(2,1)S(1)}, u32[]{:S(2)}, u32[]{:S(2)}) collective-permute-start(bf16[2,8,128,128]{3,2,1,0:T(8,128)(2,1)S(1)} %slice.14), channel_id=1, source_target_pairs={{0,4},{4,8},{8,12},{12,16},{16,20},{20,24},{24,28},{28,32},{32,36}... | collective-permute-start | bytes 1572872 | tf_op jit(solution)/shard_map/ppermute | solution.py:23
  313.5 2.6 collective-permute-start.4
  314.9 4.4 collective-permute-start.5
  330.4 3.2 copy-start.3
  428.8 6.4 %copy-start.2 = (f32[8,8,8,17,256]{4,2,3,1,0:T(8,128)S(1)}, f32[8,8,8,17,256]{4,2,3,1,0:T(8,128)}, u32[]{:S(2)}) copy-start(f32[8,8,8,17,256]{4,2,3,1,0:T(8,128)} %get-tuple-element.8) | copy-start | bytes 26738692
  441.0 74.1 %copy-start.4 = (f32[256]{0:T(256)S(1)}, f32[256]{0:T(256)}, u32[]{:S(2)}) copy-start(f32[256]{0:T(256)} %param.7) | copy-start | bytes 3076
  441.0 74.1 %copy-start.5 = (f32[256]{0:T(256)S(1)}, f32[256]{0:T(256)}, u32[]{:S(2)}) copy-start(f32[256]{0:T(256)} %param.6) | copy-start | bytes 3076
  594.6 2.5 copy-start.1
where the time goes:
time: 598 us; the launch traced here: 597 us
  waiting for transfers between devices  282 us (47%)
  blocking collectives  197 us (33%)
  local copies, waits for them, and re-layouts  51 us (9%)
  other arithmetic  32.4 us (5%)
  matrix products  19 us (3%)
  starting transfers between devices  15.6 us (3%)
    ppermute x3, waiting for transfers between devices, from_partner(): return lax.ppermute(block, axis, route)  270 us
    psum x1, blocking collectives, per_device(): group_total = lax.psum(local_sums, ('tm', 'rows'))  75.9 us
    psum x1, blocking collectives, per_device(): lax.psum(jnp.sum(centered * centered, axis=(0, 1, 2, 4)), ('tm', 'rows'))  62.4 us
    all_to_all x1, blocking collectives, per_device(): lax.all_to_all(arranged, 'tm', split_axis=1, concat_axis=2, tiled=True)  58.5 us
    conv_general_dilated x6, local copies, waits for them, and re-layouts, per_device(): lax.conv_general_dilated(padded[None], conv_weight, (1, 1, 1), 'VALID', d...  31.9 us
    conv_general_dilated x1, matrix products, per_device(): lax.conv_general_dilated(padded[None], conv_weight, (1, 1, 1), 'VALID', d...  19 us
    reshape x2, local copies, waits for them, and re-layouts, per_device(): arranged.reshape(out_height // 2, out_width // 2, out_frames, 4 * out_cha...  14.1 us
    select_n x2, other arithmetic, per_device(): jnp.where(is_upper, (partner - current) * inv_root, (current + partner) *...  12.8 us
  transfers between devices with their start and end apart: 6, of which 5 were waited for; matrix products, arithmetic and copies ran while one was open for 0% of the time, Pallas kernels for 0%

commit v1 on v0

--- a/solution.py
+++ b/solution.py
@@ -92,7 +92,10 @@
         out_frames, out_height // 2, 2, out_width // 2, 2, out_channels
     ).transpose(1, 3, 0, 2, 4, 5)
     arranged = arranged.reshape(out_height // 2, out_width // 2, out_frames, 4 * out_channels)
-    return lax.all_to_all(arranged, "tm", split_axis=1, concat_axis=2, tiled=True)
+    return jnp.concatenate(
+        lax.all_to_all(jnp.stack(jnp.split(arranged, lax.axis_size("tm"), axis=1)), "tm", 0, 0),
+        axis=2,
+    )
 
 
 def solution(mesh):

time: 598 us -> 627 us (1.048)
  local copies, waits for them, and re-layouts: 51 us -> 81.2 us
    unnamed x12 -> x43, local copies, waits for them, and re-layouts: 0.03 us -> 28.5 us
    transpose x0 -> x1, local copies, waits for them, and re-layouts: none -> 7.07 us  [per_device(): arranged = activated.reshape(out_frames, out_height // 2, 2, out_width //...]
    reshape x2 -> x1, local copies, waits for them, and re-layouts: 14.1 us -> 7.71 us  [per_device(): arranged.reshape(out_height // 2, out_width // 2, out_frames, 4 * out_cha...]
where the time goes in v1:
time: 627 us; the launch traced here: 625 us
  waiting for transfers between devices  282 us (45%)
  blocking collectives  197 us (31%)
  local copies, waits for them, and re-layouts  81.2 us (13%)
  other arithmetic  30.5 us (5%)
  matrix products  19 us (3%)
  starting transfers between devices  15.6 us (2%)
    ppermute x3, waiting for transfers between devices, from_partner(): return lax.ppermute(block, axis, route)  270 us
    psum x1, blocking collectives, per_device(): group_total = lax.psum(local_sums, ('tm', 'rows'))  75.9 us
    psum x1, blocking collectives, per_device(): lax.psum(jnp.sum(centered * centered, axis=(0, 1, 2, 4)), ('tm', 'rows'))  62.4 us
    all_to_all x1, blocking collectives, per_device(): lax.all_to_all(jnp.stack(jnp.split(arranged, lax.axis_size('tm'), axis=1)...  58.5 us
    conv_general_dilated x6, local copies, waits for them, and re-layouts, per_device(): lax.conv_general_dilated(padded[None], conv_weight, (1, 1, 1), 'VALID', d...  31.9 us
    unnamed x43, local copies, waits for them, and re-layouts  28.5 us
    conv_general_dilated x1, matrix products, per_device(): lax.conv_general_dilated(padded[None], conv_weight, (1, 1, 1), 'VALID', d...  19 us
    select_n x2, other arithmetic, per_device(): jnp.where(is_upper, (partner - current) * inv_root, (current + partner) *...  12.8 us
  transfers between devices with their start and end apart: 6, of which 5 were waited for; matrix products, arithmetic and copies ran while one was open for 0% of the time, Pallas kernels for 0%

profile of v1, /device:TPU:0, one launch (start us, length us, event | category | flops | bytes accessed | tf_op | source)
XLA Modules:
  0.0 625.4 jit_solution(4948978755118399809)
XLA Ops:
  0.0 4.3 convert_element_type.12
  4.3 3.3 collective-permute-start
  7.5 90.9 %collective-permute-done = f32[8,8,128,128]{3,2,1,0:T(8,128)} collective-permute-done((f32[8,8,128,128]{3,2,1,0:T(8,128)}, f32[8,8,128,128]{3,2,1,0:T(8,128)}, u32[]{:S(2)}, u32[]{:S(2)}) %collective-permute-start) | collective-permute-done | bytes 4194336 | tf_op jit(solution)/shard_map/ppermute | solution.py:17
  98.4 5.9 multiply_select_fusion.1
  104.3 1.5 collective-permute-start.1
  105.9 90.2 %collective-permute-done.1 = f32[8,8,128,128]{3,2,1,0:T(8,128)} collective-permute-done((f32[8,8,128,128]{3,2,1,0:T(8,128)}, f32[8,8,128,128]{3,2,1,0:T(8,128)}, u32[]{:S(2)}, u32[]{:S(2)}) %collective-permute-start.1) | collective-permute-done | bytes 4194336 | tf_op jit(solution)/shard_map/ppermute | solution.py:17
  196.1 6.9 %multiply_select_fusion = f32[8,8,128,128]{3,2,1,0:T(8,128)} fusion(f32[8,8,128,128]{3,2,1,0:T(8,128)} %multiply_select_fusion.1, f32[8,8,128,128]{3,2,1,0:T(8,128)} %collective-permute-done.1, pred[]{:T(512)S(6)} %eq.10), kind=kLoop, calls=%fused_computation.11 | loop fusion | flops 5242880 | bytes 12582913 | tf_op jit(solution)/shard_map/jit(_where)/select_n | solution.py:51
  203.0 3.0 collective-permute-start.2
  206.1 89.3 %collective-permute-done.2 = f32[8,8,128,128]{3,2,1,0:T(8,128)} collective-permute-done((f32[8,8,128,128]{3,2,1,0:T(8,128)}, f32[8,8,128,128]{3,2,1,0:T(8,128)}, u32[]{:S(2)}, u32[]{:S(2)}) %collective-permute-start.2) | collective-permute-done | bytes 4194336 | tf_op jit(solution)/shard_map/ppermute | solution.py:17
  295.4 4.5 select_convert_fusion
  299.9 5.1 collective-permute-start.3
  305.1 8.4 %collective-permute-done.3 = bf16[2,8,128,128]{3,2,1,0:T(8,128)(2,1)S(1)} collective-permute-done((bf16[2,8,128,128]{3,2,1,0:T(8,128)(2,1)S(1)}, bf16[2,8,128,128]{3,2,1,0:T(8,128)(2,1)S(1)}, u32[]{:S(2)}, u32[]{:S(2)}) %collective-permute-start.3) | collective-permute-done | bytes 524320 | tf_op jit(solution)/shard_map/ppermute | solution.py:23
  313.5 1.3 collective-permute-start.4
  314.9 1.3 collective-permute-start.5
  316.2 3.1 collective-permute-done.5
  319.3 2.1 fusion.10
  321.4 2.0 pad.5
  323.4 6.9 %reshape.27 = bf16[10,10,1,8,17,128]{5,4,3,1,0,2:T(8,128)(2,1)} reshape(bf16[10,10,1,136,128]{4,3,1,0,2:T(8,128)(2,1)} %pad.5) | data formatting | bytes 6963200 | tf_op jit(solution)/shard_map/conv_general_dilated | solution.py:60
  330.4 3.0 copy.77
  333.5 19.0 %select_reduce_fusion.1 = (f32[256]{0:T(256)S(1)}, f32[8,8,8,17,256]{4,2,3,1,0:T(8,128)}) fusion(pred[8,17]{0,1:T(8,128)(4,1)S(1)} %copy-done.3, bf16[3,3,3,128,256]{4,3,2,1,0:T(8,128)(2,1)S(1)} %copy-done, bf16[10,10,1,7,2,128]{5,3,4,1,0,2:T(8,128)(2,1)S(1)} %slice.15, bf16[10,10,1,8,17,128]{5,3,4,1,0,2:T(8,128)(2,1)S(1)} %copy.77), kind=kOutput, calls=%fused_computation.3 | convolution fusion | flops 15419842560 | bytes 14523528 | tf_op jit(solution)/shard_map/conv_general_dilated | solution.py:60
  352.8 75.9 %psum.14 = f32[32]{0:T(128)S(1)} all-reduce(f32[32]{0:T(128)S(1)} %reduce_sum.25), channel_id=1, replica_groups=mesh['tm'=32,'rows'=4] {'tm','rows'}, use_global_device_ids=true, to_apply=%region_2.3 | all-reduce | flops 32 | bytes 256 | tf_op jit(solution)/shard_map/psum | solution.py:82
  428.9 6.3 %copy.78 = f32[8,8,8,17,256]{4,1,3,2,0:T(8,128)S(1)} copy(f32[8,8,8,17,256]{4,2,3,1,0:T(8,128)} %get-tuple-element.8) | data formatting | bytes 17825792 | tf_op jit(solution)/shard_map/conv_general_dilated | solution.py:60
  435.2 1.5 select_reduce_fusion
  436.8 4.1 slice.16
  441.0 11.5 %copy.79 = f32[8,8,1,128,256]{4,0,3,1,2:T(8,128)} copy(f32[8,8,1,128,256]{4,1,3,0,2:T(8,128)} %slice.16) | data formatting | bytes 16777216 | tf_op jit(solution)/shard_map/conv_general_dilated | solution.py:60
  452.5 62.4 %psum.15 = f32[32]{0:T(128)S(1)} all-reduce(f32[32]{0:T(128)S(1)} %reduce_sum.37), channel_id=1, replica_groups=mesh['tm'=32,'rows'=4] {'tm','rows'}, use_global_device_ids=true, to_apply=%region_5.6 | all-reduce | flops 32 | bytes 256 | tf_op jit(solution)/shard_map/psum | solution.py:85
  515.2 5.0 fusion.2
  520.1 7.1 %copy.80 = bf16[4,64,8,2,2,256]{5,4,3,2,1,0:T(2,128)(2,1)} copy(bf16[4,64,8,2,2,256]{5,2,4,1,3,0:T(8,128)(2,1)S(1)} %fusion.2) | data formatting | bytes 8388608 | tf_op jit(solution)/shard_map/transpose | solution.py:93
  527.2 7.7 %reshape.22 = bf16[4,64,8,1024]{3,2,1,0:T(8,128)(2,1)} reshape(bf16[4,64,8,2,2,256]{5,4,3,2,1,0:T(2,128)(2,1)} %copy.80) | data formatting | bytes 8388608 | tf_op jit(solution)/shard_map/reshape | solution.py:94
  535.8 0.9 fusion.47
  537.7 0.9 fusion.45
  539.5 0.9 fusion.43
  540.4 0.9 fusion.42
  542.3 0.9 fusion.40
  544.1 0.9 fusion.38
  545.1 0.9 fusion.37
  546.0 0.9 fusion.36
  546.9 0.9 fusion.35
  548.7 0.9 fusion.33
  550.6 0.9 fusion.31
  551.5 0.9 fusion.30
  552.4 0.9 fusion.29
  553.4 0.9 fusion.28
  555.2 0.9 fusion.26
  557.0 0.9 fusion.24
  558.0 0.9 fusion.23
  564.4 58.5 %all_to_all.5 = bf16[32,4,2,8,1024]{4,3,2,1,0:T(8,128)(2,1)S(1)} all-to-all(bf16[32,4,2,8,1024]{4,3,2,1,0:T(8,128)(2,1)S(1)} %fusion.17), channel_id=1, replica_groups=mesh['tm'=32,'rows'=4] {'tm'}, dimensions={0} | all-to-all | bytes 8388608 | tf_op jit(solution)/shard_map/all_to_all | solution.py:96
  622.9 2.5 copy_bitcast_fusion
  (41 shorter events, 14.8 us)
Async XLA Ops:
  0.0 333.5 %copy-start = (bf16[3,3,3,128,256]{4,3,2,1,0:T(8,128)(2,1)S(1)}, bf16[3,3,3,128,256]{4,3,2,1,0:T(8,128)(2,1)}, u32[]{:S(2)}) copy-start(bf16[3,3,3,128,256]{4,3,2,1,0:T(8,128)(2,1)} %param.5) | copy-start | bytes 5308420
  4.3 94.2 %collective-permute-start = (f32[8,8,128,128]{3,2,1,0:T(8,128)}, f32[8,8,128,128]{3,2,1,0:T(8,128)}, u32[]{:S(2)}, u32[]{:S(2)}) collective-permute-start(f32[8,8,128,128]{3,2,1,0:T(8,128)} %convert_element_type.12), channel_id=1, source_target_pairs={{0,4},{4,0},{8,12},{12,8},{16,20},{20,16},{24,28},{28,24},{32,36},... | collective-permute-start | bytes 12582920 | tf_op jit(solution)/shard_map/ppermute | solution.py:17
  104.3 91.8 %collective-permute-start.1 = (f32[8,8,128,128]{3,2,1,0:T(8,128)}, f32[8,8,128,128]{3,2,1,0:T(8,128)}, u32[]{:S(2)}, u32[]{:S(2)}) collective-permute-start(f32[8,8,128,128]{3,2,1,0:T(8,128)} %multiply_select_fusion.1), channel_id=1, source_target_pairs={{0,8},{8,0},{4,12},{12,4},{16,24},{24,16},{20,28},{28,20},{32,40},... | collective-permute-start | bytes 12582920 | tf_op jit(solution)/shard_map/ppermute | solution.py:17
  203.0 92.4 %collective-permute-start.2 = (f32[8,8,128,128]{3,2,1,0:T(8,128)}, f32[8,8,128,128]{3,2,1,0:T(8,128)}, u32[]{:S(2)}, u32[]{:S(2)}) collective-permute-start(f32[8,8,128,128]{3,2,1,0:T(8,128)} %multiply_select_fusion), channel_id=1, source_target_pairs={{0,16},{16,0},{4,20},{20,4},{8,24},{24,8},{12,28},{28,12},{32,48},... | collective-permute-start | bytes 12582920 | tf_op jit(solution)/shard_map/ppermute | solution.py:17
  299.9 13.5 %collective-permute-start.3 = (bf16[2,8,128,128]{3,2,1,0:T(8,128)(2,1)S(1)}, bf16[2,8,128,128]{3,2,1,0:T(8,128)(2,1)S(1)}, u32[]{:S(2)}, u32[]{:S(2)}) collective-permute-start(bf16[2,8,128,128]{3,2,1,0:T(8,128)(2,1)S(1)} %slice.14), channel_id=1, source_target_pairs={{0,4},{4,8},{8,12},{12,16},{16,20},{20,24},{24,28},{28,32},{32,36}... | collective-permute-start | bytes 1572872 | tf_op jit(solution)/shard_map/ppermute | solution.py:23
  313.5 2.6 collective-permute-start.4
  314.9 4.4 collective-permute-start.5
  330.4 3.2 copy-start.3
  428.8 6.4 %copy-start.2 = (f32[8,8,8,17,256]{4,2,3,1,0:T(8,128)S(1)}, f32[8,8,8,17,256]{4,2,3,1,0:T(8,128)}, u32[]{:S(2)}) copy-start(f32[8,8,8,17,256]{4,2,3,1,0:T(8,128)} %get-tuple-element.8) | copy-start | bytes 26738692
  441.0 74.1 %copy-start.4 = (f32[256]{0:T(256)S(1)}, f32[256]{0:T(256)}, u32[]{:S(2)}) copy-start(f32[256]{0:T(256)} %param.7) | copy-start | bytes 3076
  441.0 74.1 %copy-start.5 = (f32[256]{0:T(256)S(1)}, f32[256]{0:T(256)}, u32[]{:S(2)}) copy-start(f32[256]{0:T(256)} %param.6) | copy-start | bytes 3076
  564.4 60.9 %copy-start.1 = (bf16[3,3,3,128,256]{4,3,2,1,0:T(8,128)(2,1)S(1)}, bf16[3,3,3,128,256]{4,3,2,1,0:T(8,128)(2,1)}, u32[]{:S(2)}) copy-start(bf16[3,3,3,128,256]{4,3,2,1,0:T(8,128)(2,1)} %param.5) | copy-start | bytes 5308420
